TPU v7x, 32 devices: a whole 2x2x4 slice. The times are simulated.
32 devices in a mesh: section: 2 (over y), expert: 16 (over z, x, core).
Axes of the slice: x: 2, y: 2, z: 4, core: 2. Of those that a mesh axis runs over, the one named last changes fastest.
Arguments:
- section_input: bfloat16 [2, 2048, 2880], P('section', 'expert'), may hold values from -6 to 6
- attention_gain: float32 [2, 2880], P('section'), may hold values from 0.1 to 1.9
- query_key_value_weight: bfloat16 [2, 2880, 2560], P('section', 'expert'), may hold values from -0.109375 to 0.109375
- qkv_bias: float32 [2, 2560], P('section'), may hold values from -3 to 8
- out_weight: bfloat16 [2, 2048, 2880], P('section'), may hold values from -0.125 to 0.125
- out_bias: float32 [2, 2880], P('section'), may hold values from -3 to 3
- attention_sink_logits: float32 [2, 32], P('section'), may hold values from -1 to 250
- expert_gain: float32 [2, 2880], P('section'), may hold values from 0.1 to 1.9
- gate_up_weight: bfloat16 [2, 16, 2880, 1440], P('section', 'expert'), may hold values from -0.109375 to 0.109375
- down_weight: bfloat16 [2, 16, 720, 2880], P('section', 'expert'), may hold values from -0.15625 to 0.15625
- expert_ids: int32 [2, 2048, 4], P('section', 'expert'), may hold values from 0 to 7, all different within a row; in each aligned block of 128 rows (0 to 127, 128 to 255, ..., all dimensions but the last counted through in order) at most 80 rows name the same one
- gate_logits: float32 [2, 2048, 4], P('section', 'expert'), may hold values from -8 to 204
- placement: int32 [2, 8], P('section'), may hold values from 0 to 7, each once within a row
Outputs:
- section_output: bfloat16 [2, 2048, 2880], P('section', 'expert')
Inputs may be any that keep to these rules, and one draw needn't show every extreme that they name: `expert_ids`: within each section, among the 128 tokens of one device no expert is named more than 80 times, a bound that some block reaches. `placement`: each row names every expert once.
All inputs are finite; a program needn't handle non-finite values.
Results may differ from a plain program's by a relative error of at most 0.018.
Values may be sent and summed in bfloat16 or wider, within the bound.
No kernel may reach another device: no remote copies, remote signals or barrier semaphores. Data moves between devices by JAX's collectives and lax.ppermute only.
A program may use at most 128 MiB of HBM per device.

v0:
```python
import jax
import jax.numpy as jnp
from jax import lax
from jax.sharding import PartitionSpec as P

HEAD_DIM = 64
QUERY_HEADS = 32
KEY_VALUE_HEADS = 4
WINDOW_TOKENS = 128
TOP = 4


def from_behind(x, axis, by):
    size = lax.axis_size(axis)
    pairs = [(i, i + by) for i in range(size) if 0 <= i + by < size]
    return lax.ppermute(x, axis, pairs)


def passed_along(x, axis, by):
    size = lax.axis_size(axis)
    return lax.ppermute(x, axis, [(i, (i + by) % size) for i in range(size)])


def normed(vector, gain_row):
    as_float = vector.astype(jnp.float32)
    inverse_rms = lax.rsqrt(jnp.mean(as_float * as_float, axis=-1, keepdims=True) + 1e-05)
    return (as_float * inverse_rms * gain_row).astype(jnp.bfloat16)


def swiglu(hidden):
    half_cols = hidden.shape[1] // 2
    gate_part = hidden[:, :half_cols]
    up_part = hidden[:, half_cols:]
    return ((up_part + 1.0) * gate_part * jax.nn.sigmoid(1.702 * gate_part)).astype(jnp.bfloat16)


def shards(
    section_input,
    attention_gain,
    query_key_value_weight,
    qkv_bias,
    out_weight,
    out_bias,
    attention_sink_logits,
    expert_gain,
    gate_up_weight,
    down_weight,
    expert_ids,
    gate_logits,
    placement,
):
    count_of_rows = section_input.shape[1]
    model_width = section_input.shape[2]
    experts_count = placement.shape[1]
    slot_count = 2 * min(count_of_rows // 2, count_of_rows * TOP * 5 // (8 * experts_count))
    offset = lax.axis_index("expert") * count_of_rows
    query_group_width = QUERY_HEADS // KEY_VALUE_HEADS
    tile_gu = gate_up_weight[0, 0]
    tile_down = down_weight[0, 0]
    state = section_input[0]
    normed_in = normed(state, attention_gain[0])
    projected_rows = (
        jnp.dot(
            normed_in,
            lax.all_gather(query_key_value_weight[0], "expert", axis=0, tiled=True),
            preferred_element_type=jnp.float32,
        )
        + qkv_bias[0]
    ).astype(jnp.bfloat16)
    query_rows = projected_rows[:, : QUERY_HEADS * HEAD_DIM].reshape(
        count_of_rows, KEY_VALUE_HEADS, query_group_width, HEAD_DIM
    )
    key_value = projected_rows[:, QUERY_HEADS * HEAD_DIM :]
    rim_rows = from_behind(key_value, "expert", 1)
    rows_in_window = jnp.concatenate([rim_rows, key_value], 0)
    key_row_slice = rows_in_window[:, : KEY_VALUE_HEADS * HEAD_DIM].reshape(
        WINDOW_TOKENS + count_of_rows, KEY_VALUE_HEADS, HEAD_DIM
    )
    value_row_slice = rows_in_window[:, KEY_VALUE_HEADS * HEAD_DIM :].reshape(
        WINDOW_TOKENS + count_of_rows, KEY_VALUE_HEADS, HEAD_DIM
    )
    scores = (
        jnp.einsum("ikgd,jkd->kgij", query_rows, key_row_slice, preferred_element_type=jnp.float32)
        * 0.125
    )
    query_pos = offset + jnp.arange(count_of_rows, dtype=jnp.int32)
    key_pos = offset - WINDOW_TOKENS + jnp.arange(WINDOW_TOKENS + count_of_rows, dtype=jnp.int32)
    distance = query_pos[:, None] - key_pos[None, :]
    inside = (distance >= 0) & (distance < WINDOW_TOKENS) & (key_pos >= 0)[None, :]
    head_sink_logit = attention_sink_logits[0].reshape(KEY_VALUE_HEADS, query_group_width)[
        :, :, None
    ]
    masked = jnp.where(inside, scores, -1e30)
    peak = jnp.maximum(jnp.max(masked, axis=-1), head_sink_logit)
    numer = jnp.where(inside, jnp.exp(masked - peak[..., None]), 0.0)
    denominator = jnp.sum(numer, axis=-1) + jnp.exp(head_sink_logit - peak)
    attention = (numer / denominator[..., None]).astype(jnp.bfloat16)
    mixed = jnp.einsum(
        "kgij,jkd->ikgd", attention, value_row_slice, preferred_element_type=jnp.float32
    )
    attended = mixed.astype(jnp.bfloat16).reshape(count_of_rows, QUERY_HEADS * HEAD_DIM)
    residual = (
        state.astype(jnp.float32)
        + jnp.dot(attended, out_weight[0], preferred_element_type=jnp.float32)
        + out_bias[0]
    ).astype(jnp.bfloat16)
    normed_mid = normed(residual, expert_gain[0])
    flat_ids = expert_ids[0].reshape(-1)
    expert_range = jnp.arange(experts_count, dtype=jnp.int32)
    one_hot = (flat_ids[:, None] == expert_range[None, :]).astype(jnp.int32)
    slot_of = jnp.sum((jnp.cumsum(one_hot, axis=0) - 1) * one_hot, axis=-1)
    token_of = jnp.arange(count_of_rows * TOP, dtype=jnp.int32) // TOP
    source_rows = (
        jnp.full((experts_count * slot_count,), -1, jnp.int32)
        .at[flat_ids * slot_count + slot_of]
        .set(token_of)
    )
    valid_rows = (source_rows >= 0)[:, None].astype(jnp.bfloat16)
    gathered = jnp.take(normed_mid, jnp.maximum(source_rows, 0), axis=0) * valid_rows
    by_expert = gathered.reshape(experts_count, slot_count, model_width)
    holders = placement[0]
    by_pair = jnp.take(by_expert, holders, axis=0)
    matches = (holders[:, None] == expert_range[None, :]).astype(jnp.int32)
    holder_of = jnp.sum(expert_range[:, None] * matches, axis=0)
    outgoing = jnp.repeat(by_pair, 2, axis=0)
    rows_in = lax.all_to_all(outgoing, "expert", split_axis=0, concat_axis=0, tiled=True)
    in_shape = rows_in.shape
    hidden = jnp.dot(rows_in.reshape(-1, model_width), tile_gu, preferred_element_type=jnp.float32)
    returned = lax.all_to_all(
        jnp.dot(swiglu(hidden), tile_down, preferred_element_type=jnp.float32)
        .astype(jnp.bfloat16)
        .reshape(in_shape),
        "expert",
        split_axis=0,
        concat_axis=0,
        tiled=True,
    )
    paired = returned.astype(jnp.float32).reshape(experts_count, 2, slot_count, model_width)
    summed = (
        (paired[:, 0] + paired[:, 1])
        .astype(jnp.bfloat16)
        .reshape(experts_count * slot_count, model_width)
    )
    picked = jnp.take(summed, holder_of[flat_ids] * slot_count + slot_of, axis=0).reshape(
        count_of_rows, TOP, model_width
    )
    picked = lax.optimization_barrier(picked).astype(jnp.float32)
    gate_weights = jax.nn.softmax(gate_logits[0], axis=-1)
    fresh = (
        residual.astype(jnp.float32) + jnp.sum(picked * gate_weights[..., None], axis=1)
    ).astype(jnp.bfloat16)
    moved = passed_along(fresh, "section", 1)
    return moved[None]


def solution(mesh):
    return jax.shard_map(
        shards,
        mesh=mesh,
        in_specs=(
            P("section", "expert", None),
            P("section", None),
            P("section", "expert", None),
            P("section", None),
            P("section", None, None),
            P("section", None),
            P("section", None),
            P("section", None),
            P("section", "expert", None, None),
            P("section", "expert", None, None),
            P("section", "expert", None),
            P("section", "expert", None),
            P("section", None),
        ),
        out_specs=P("section", "expert", None),
        check_vma=False,
    )
```

profile of v0, /device:TPU:10, one launch (start us, length us, event | category | flops | bytes accessed | tf_op | source)
XLA Modules:
  0.0 655.5 jit_solution(10432839665436297270)
XLA Ops:
  6.6 4.0 copy.62
  11.1 1.1 reduce-window.6
  13.5 4.4 compare_select_fusion.4
  18.5 2.4 scatter_custom_fusion
  21.6 138.9 %all-gather.3.cloned.1.call-done = bf16[1,2880,2560]{2,0,1:T(2,128)(2,1)} async-done(((bf16[1,180,2560]{2,0,1:T(2,128)(2,1)}), bf16[1,2880,2560]{2,0,1:T(2,128)(2,1)}) %all-gather.3.cloned.1.call-update) | async-done | bytes 14745616 | tf_op jit(solution)/shard_map/all_gather | solution.py:65
  160.5 15.2 %fusion.17 = bf16[128,2560]{1,0:T(8,128)(2,1)S(1)} fusion(bf16[1,2880,2560]{2,0,1:T(2,128)(2,1)} %all-gather.3.cloned.1.call-done, bf16[1,128,2880]{1,2,0:T(8,128)(2,1)S(1)} %copy-done.2, f32[2880]{0:T(1024)S(1)} %reduce.1, f32[128]{0:T(128)S(1)} %add_rsqrt_fusion.1, f32[2560]{0:T(1024)S(1)} %reduce.2), kind=kOutput, calls=%fused_computation.29 | convolution fusion | flops 1889566720 | bytes 16160512 | tf_op jit(solution)/shard_map/dot_general | solution.py:63
  175.8 2.3 collective-permute-start
  180.0 2.1 collective-permute-done
  184.3 1.3 fusion.40
  185.6 1.2 slice-done.1
  187.8 3.3 multiply_reduce_fusion.1
  191.1 1.1 copy-done
  193.0 4.6 gather_fusion
  197.6 4.5 select_multiply_fusion
  202.1 4.9 gather_fusion.1
  206.9 2.5 broadcast_select_fusion
  210.0 170.1 %all_to_all.10 = bf16[16,80,2880]{2,1,0:T(8,128)(2,1)S(1)} all-to-all(bf16[16,80,2880]{2,1,0:T(8,128)(2,1)S(1)} %bitcast.119), channel_id=1, replica_groups=mesh['section'=2,'expert'=16] {'expert'}, dimensions={0} | all-to-all | bytes 14745600 | tf_op jit(solution)/shard_map/all_to_all | solution.py:126
  380.1 15.5 %fusion.5 = f32[1280,1440]{0,1:T(8,128)} fusion(bf16[1280,2880]{1,0:T(8,128)(2,1)S(1)} %bitcast.121, bf16[1,1,2880,1440]{2,3,1,0:T(8,128)(2,1)} %param.21), kind=kOutput, calls=%fused_computation.10 | convolution fusion | flops 10616832000 | bytes 23040000 | tf_op jit(solution)/shard_map/dot_general | solution.py:128
  395.6 11.9 %convolution_convert_fusion = bf16[1280,2880]{0,1:T(8,128)(2,1)} fusion(bf16[1,1,720,2880]{3,2,1,0:T(8,128)(2,1)S(1)} %bitcast.134, f32[1280,1440]{0,1:T(8,128)} %fusion.5), kind=kOutput, calls=%fused_computation.9 | convolution fusion | flops 5319475200 | bytes 18892800 | tf_op jit(solution)/shard_map/dot_general | solution.py:130
  407.5 10.4 %copy.71 = bf16[1280,2880]{1,0:T(8,128)(2,1)} copy(bf16[1280,2880]{0,1:T(8,128)(2,1)} %convolution_convert_fusion) | data formatting | bytes 14745600 | tf_op jit(solution)/shard_map/convert_element_type | solution.py:131
  417.9 6.1 all-to-all-start.1
  424.4 163.6 %all-to-all-done.1 = bf16[16,80,2880]{2,1,0:T(8,128)(2,1)} async-done(((bf16[16,80,2880]{2,1,0:T(8,128)(2,1)}), bf16[16,80,2880]{2,1,0:T(8,128)(2,1)}, u32[]{:S(2)}, u32[]{:S(2)}) %all-to-all-start.1) | async-done | bytes 7372832 | tf_op jit(solution)/shard_map/all_to_all | solution.py:129
  588.0 9.5 %convert.4 = f32[8,2,80,2880]{3,2,1,0:T(8,128)} convert(bf16[8,2,80,2880]{3,2,1,0:T(8,128)(2,1)} %bitcast.36) | non-fusion elementwise | flops 3686400 | bytes 22118400 | tf_op jit(solution)/shard_map/reshape | solution.py:138
  597.6 7.8 %fusion.8 = bf16[8,1,80,2880]{3,2,0,1:T(8,128)(2,1)} fusion(f32[8,2,80,2880]{3,2,1,0:T(8,128)} %convert.4), kind=kLoop, calls=%fused_computation.14 | loop fusion | flops 3686400 | bytes 18432000 | tf_op jit(solution)/shard_map/convert_element_type | solution.py:141
  605.4 9.3 %gather_fusion.2 = bf16[512,2880]{1,0:T(8,128)(2,1)} fusion(bf16[640,2880]{1,0:T(8,128)(2,1)} %bitcast.117, s32[1024]{0:T(1024)S(1)} %pad_clamp_fusion), kind=kCustom, calls=%fused_computation.2 | custom fusion | bytes 5900288 | tf_op jit(solution)/shard_map/jit(_take)/gather | solution.py:144
  614.6 4.9 gather.24
  619.6 1.4 broadcast_select_fusion.1
  621.0 4.5 multiply_reduce_fusion
  625.5 1.6 copy.75
  627.1 1.5 add_convert_fusion
  628.6 1.6 collective-permute-start.1
  630.1 17.2 %collective-permute-done.1 = bf16[128,2880]{0,1:T(8,128)(2,1)S(1)} collective-permute-done((bf16[128,2880]{0,1:T(8,128)(2,1)S(1)}, bf16[128,2880]{0,1:T(8,128)(2,1)S(1)}, u32[]{:S(2)}, u32[]{:S(2)}) %collective-permute-start.1) | collective-permute-done | bytes 737312 | tf_op jit(solution)/shard_map/ppermute | solution.py:21
  (92 shorter events, 10.5 us)
Async XLA Ops:
  6.5 4.0 copy-start.8
  6.5 4.5 copy-start.4
  6.5 4.5 copy-start.7
  6.5 6.0 copy-start.9
  6.5 14.5 %copy-start.2 = (bf16[1,128,2880]{1,2,0:T(8,128)(2,1)S(1)}, bf16[1,128,2880]{1,2,0:T(8,128)(2,1)}, u32[]{:S(2)}) copy-start(bf16[1,128,2880]{1,2,0:T(8,128)(2,1)} %param.13) | copy-start | bytes 2211844
  6.5 154.0 %all-gather.3.cloned.1.call-start = ((), (), s32[]{:S(2)}) async-start(), calls=%async_computation.2 | async-start | bytes 31334400 | tf_op jit(solution)/shard_map/all_gather | solution.py:65
  21.6 156.5 %copy-start.5 = (f32[1,2880]{1,0:T(1,128)S(1)}, f32[1,2880]{1,0:T(1,128)}, u32[]{:S(2)}) copy-start(f32[1,2880]{1,0:T(1,128)} %param.18) | copy-start | bytes 34564
  21.6 157.1 %copy-start.10 = (f32[1,32]{1,0:T(1,128)S(1)}, f32[1,32]{1,0:T(1,128)}, u32[]{:S(2)}) copy-start(f32[1,32]{1,0:T(1,128)} %param.19) | copy-start | bytes 388
  21.6 157.8 %copy-start.6 = (f32[1,2880]{1,0:T(1,128)S(1)}, f32[1,2880]{1,0:T(1,128)}, u32[]{:S(2)}) copy-start(f32[1,2880]{1,0:T(1,128)} %param.20) | copy-start | bytes 34564
  175.8 6.3 collective-permute-start
  183.1 2.5 slice-start
  184.3 2.5 slice-start.1
  184.3 3.5 slice-start.2
  191.1 1.2 copy-start
  210.0 185.6 %slice-start.3 = ((s8[4239360]{0:T(1024)(128)(4,1)}), s8[45056]{0:T(1024)(128)(4,1)S(1)}, s32[]{:S(2)}) async-start(s8[4239360]{0:T(1024)(128)(4,1)} %bitcast.133), calls=%async_computation.6 | async-start | bytes 90112
  380.1 15.5 %slice-start.4 = ((s8[4239360]{0:T(1024)(128)(4,1)}), s8[4194304]{0:T(1024)(128)(4,1)S(1)}, s32[]{:S(2)}) async-start(s8[4239360]{0:T(1024)(128)(4,1)} %bitcast.133), calls=%async_computation.7 | async-start | bytes 8388608
  417.9 6.3 copy-start.3
  417.9 170.1 %all-to-all-start.1 = ((bf16[16,80,2880]{2,1,0:T(8,128)(2,1)}), bf16[16,80,2880]{2,1,0:T(8,128)(2,1)}, u32[]{:S(2)}, u32[]{:S(2)}) async-start(bf16[16,80,2880]{2,1,0:T(8,128)(2,1)} %bitcast.118), calls=%async_computation.1 | async-start | bytes 15073280 | tf_op jit(solution)/shard_map/all_to_all | solution.py:129
  621.0 6.1 copy-start.1
  628.6 18.8 %collective-permute-start.1 = (bf16[128,2880]{0,1:T(8,128)(2,1)S(1)}, bf16[128,2880]{0,1:T(8,128)(2,1)S(1)}, u32[]{:S(2)}, u32[]{:S(2)}) collective-permute-start(bf16[128,2880]{0,1:T(8,128)(2,1)S(1)} %add_convert_fusion), channel_id=1, source_target_pairs={{0,16},{16,0},{1,17},{17,1},{2,18},{18,2},{3,19},{19,3},{4,20},{20... | collective-permute-start | bytes 2211848 | tf_op jit(solution)/shard_map/ppermute | solution.py:21
Sparse Core Ops, SparseCore 0:
  10.7 149.7 all-gather.2
where the time goes:
time: 663 us; the launch traced here: 655 us
  waiting for transfers between devices  322 us (49%)
  blocking collectives  170 us (26%)
  local copies, waits for them, and re-layouts  50 us (8%)
  matrix products  47.9 us (7%)
  other arithmetic  41.3 us (6%)
  between operations  14.3 us (2%)
  starting transfers between devices  10.1 us (2%)
    all_to_all x1, blocking collectives, shards(): lax.all_to_all(outgoing, 'expert', split_axis=0, concat_axis=0, tiled=True)  170 us
    all_to_all x1, waiting for transfers between devices, shards(): lax.all_to_all(jnp.dot(swiglu(hidden), tile_down, preferred_element_type=...  164 us
    all_gather x1, waiting for transfers between devices, shards(): lax.all_gather(query_key_value_weight[0], 'expert', axis=0, tiled=True)  139 us
    ppermute x1, waiting for transfers between devices, passed_along(): return lax.ppermute(x, axis, [(i, (i + by) % size) for i in range(size)])  17.2 us
    dot_general x1, matrix products, shards(): jnp.dot(rows_in.reshape(-1, model_width), tile_gu, preferred_element_type...  15.5 us
    dot_general x1, matrix products, shards(): jnp.dot(normed_in, lax.all_gather(query_key_value_weight[0], 'expert', ax...  15.2 us
    gather x2, local copies, waits for them, and re-layouts, shards(): jnp.take(summed, holder_of[flat_ids] * slot_count + slot_of, axis=0)  14.2 us
  transfers between devices with their start and end apart: 4, of which 4 were waited for; matrix products, arithmetic and copies ran while one was open for 2% of the time, Pallas kernels for 0%

commit v1 on v0

v1 whole, which is shorter than its diff:
```python
import functools

import jax
import jax.numpy as jnp
from jax import lax
from jax.experimental import pallas as pl
from jax.experimental.pallas import tpu as pltpu
from jax.sharding import PartitionSpec as P

HEAD_DIM = 64
QUERY_HEADS = 32
KEY_VALUE_HEADS = 4
WINDOW_TOKENS = 128
TOP = 4
GROUP = QUERY_HEADS // KEY_VALUE_HEADS
QUERY_COLS = GROUP * HEAD_DIM
GROUP_COLS = QUERY_COLS + 2 * HEAD_DIM
BF16 = jnp.bfloat16
F32 = jnp.float32
VMEM_BYTES = 50 * 1024 * 1024


def swap(x, mask):
    size = lax.axis_size("expert")
    return lax.ppermute(x, "expert", [(i, i ^ mask) for i in range(size)])


def normed(vector, gain_row):
    as_float = vector.astype(F32)
    inverse_rms = lax.rsqrt(jnp.mean(as_float * as_float, axis=-1, keepdims=True) + 1e-05)
    return (as_float * inverse_rms * gain_row).astype(BF16)


def params(limit=VMEM_BYTES):
    return pltpu.CompilerParams(vmem_limit_bytes=limit)


SMEM_SPEC = pl.BlockSpec(memory_space=pltpu.SMEM)
VMEM_SPEC = pl.BlockSpec(memory_space=pltpu.VMEM)


def project_half(which, own, core, first, tokens, mine, theirs, depth):
    total = None
    for r in range(4):
        first_core = jnp.where(core == 0, mine[r], theirs[r])
        second_core = jnp.where(core == 0, theirs[r], mine[r])
        both = jnp.concatenate([first_core, second_core], axis=0)
        start = pl.multiple_of((which * 4 + (own ^ r)) * 2 * depth, 128)
        columns = pl.ds(start, 2 * depth)
        stacked = jnp.concatenate([t[:, columns] for t in tokens], axis=0)
        part = jnp.dot(stacked, both, preferred_element_type=F32)
        total = part if total is None else total + part
    return total if first is None else total + first


def project_near(depth, where, t0, t1, t2, t3, mine, theirs, out):
    half, own, core = where[0], where[1], where[2]
    out[...] = project_half(half, own, core, None, (t0, t1, t2, t3), mine, theirs, depth)


def project_far(depth, where, t0, t1, t2, t3, mine, theirs, near, bias, queries, keyvals):
    half, own, core = where[0], where[1], where[2]
    total = project_half(
        1 - half, own, core, near[...], (t0, t1, t2, t3), mine, theirs, depth
    )
    rows = t0.shape[0]
    projected = (total + bias[pl.ds(own, 1), :]).astype(BF16)
    for r in range(4):
        block = projected[r * rows : (r + 1) * rows]
        queries[own ^ r] = block[:, :QUERY_COLS]
        keyvals[own ^ r] = block[:, QUERY_COLS:]


def attend(where, queries, keyvals, behind, sinks, out):
    half, own, core = where[0], where[1], where[2]
    rows = queries.shape[1]
    keys = 2 * rows
    shape = (GROUP * rows, keys)
    query_at = lax.rem(lax.broadcasted_iota(jnp.int32, shape, 0), rows)
    distance = query_at - lax.broadcasted_iota(jnp.int32, shape, 1) + rows
    band = (distance >= 0) & (distance < WINDOW_TOKENS)
    sink = jnp.concatenate(
        [jnp.full((rows, 1), sinks[own * GROUP + j], F32) for j in range(GROUP)], axis=0
    )
    for b in range(4):
        before = behind[b + core]
        now = keyvals[b]
        both = jnp.concatenate([before, now], axis=0)
        q = queries[b]
        stacked = jnp.concatenate(
            [q[:, j * HEAD_DIM : (j + 1) * HEAD_DIM] for j in range(GROUP)], axis=0
        )
        scores = (
            lax.dot_general(
                stacked,
                both[:, :HEAD_DIM],
                (((1,), (1,)), ((), ())),
                preferred_element_type=F32,
            )
            * 0.125
        )
        inside = band
        inside = band
        if b == 0:
            first_key = jnp.where((half == 0) & (core == 0), rows, 0)
            inside = band & (lax.broadcasted_iota(jnp.int32, shape, 1) >= first_key)
        masked = jnp.where(inside, scores, -1e30)
        peak = jnp.maximum(jnp.max(masked, axis=-1, keepdims=True), sink)
        numer = jnp.where(inside, jnp.exp(masked - peak), 0.0)
        denominator = jnp.sum(numer, axis=-1, keepdims=True) + jnp.exp(sink - peak)
        weights = (numer / denominator).astype(BF16)
        mixed = jnp.dot(weights, both[:, HEAD_DIM:], preferred_element_type=F32).astype(BF16)
        out[b] = jnp.concatenate(
            [mixed[j * rows : (j + 1) * rows] for j in range(GROUP)], axis=1
        )


def out_project(where, attended, weight, state, bias, gain, residual, mid, total):
    step = pl.program_id(0)

    @pl.when(step == 0)
    def _():
        total[...] = state[...].astype(F32) + bias[...]

    total[...] += jnp.dot(attended[0], weight[...], preferred_element_type=F32)

    @pl.when(step == 3)
    def _():
        kept = total[...].astype(BF16)
        residual[...] = kept
        mid[...] = normed(kept, gain[...])


def routing(ids, logits, experts, slots):
    gates = jax.nn.softmax(logits, axis=-1)
    hits = ids[None, :, :] == experts[:, None, None]
    chosen = jnp.any(hits, axis=-1)
    weight = jnp.sum(jnp.where(hits, gates[None], 0.0), axis=-1)
    rows = ids.shape[0]
    earlier = jnp.arange(rows)[:, None] < jnp.arange(rows)[None, :]
    rank = jnp.dot(chosen.astype(BF16), earlier.astype(BF16), preferred_element_type=F32)
    slot = jnp.arange(slots, dtype=jnp.int32)
    one_hot = (rank.astype(jnp.int32)[:, None, :] == slot[None, :, None]) & chosen[:, None, :]
    return one_hot.astype(BF16), weight


def packed(one_hot, rows):
    return jnp.einsum("rst,td->rsd", one_hot, rows, preferred_element_type=F32).astype(BF16)


def unpacked(one_hot, weight, results):
    spread = jnp.einsum("rst,rsd->rtd", one_hot, results, preferred_element_type=F32)
    return jnp.sum(spread * weight[:, :, None], axis=0)


def swiglu(hidden):
    half_cols = hidden.shape[1] // 2
    gate_part = hidden[:, :half_cols]
    up_part = hidden[:, half_cols:]
    return ((up_part + 1.0) * gate_part * jax.nn.sigmoid(1.702 * gate_part)).astype(BF16)


def expert(rows, tiles):
    shape = rows.shape
    flat = rows.reshape(-1, shape[-1])
    total = 0.0
    for gate_up, down in tiles:
        hidden = jnp.dot(flat, gate_up, preferred_element_type=F32)
        part = jnp.dot(swiglu(hidden), down, preferred_element_type=F32).astype(BF16)
        total = total + part.astype(F32)
    return total.astype(BF16).reshape(shape)


def spread_out(blocks):
    return [blocks[0]] + [swap(blocks[r], 2 * r) for r in range(1, 4)]


def shards(
    section_input,
    attention_gain,
    query_key_value_weight,
    qkv_bias,
    out_weight,
    out_bias,
    attention_sink_logits,
    expert_gain,
    gate_up_weight,
    down_weight,
    expert_ids,
    gate_logits,
    placement,
):
    rows, width = section_input.shape[1:]
    experts_count = placement.shape[1]
    slots = 2 * min(rows // 2, rows * TOP * 5 // (8 * experts_count))
    me = lax.axis_index("expert").astype(jnp.int32)
    half, own, core = me >> 3, (me >> 1) & 3, me & 1
    where = jnp.stack([half, own, core])
    state = section_input[0]

    weight = query_key_value_weight[0]
    weight_rows = weight.shape[0]
    depth = -(-weight_rows // 64) * 64
    query_end = QUERY_HEADS * HEAD_DIM
    key_end = query_end + KEY_VALUE_HEADS * HEAD_DIM

    def grouped(array):
        lead = array.shape[0]
        return jnp.concatenate(
            [
                array[:, :query_end].reshape(lead, 4, QUERY_COLS),
                array[:, query_end:key_end].reshape(lead, 4, HEAD_DIM),
                array[:, key_end:].reshape(lead, 4, HEAD_DIM),
            ],
            axis=2,
        )

    by_group = jnp.pad(grouped(weight).transpose(1, 0, 2), ((0, 0), (0, depth - weight_rows), (0, 0)))
    bias = grouped(qkv_bias)[0]
    pick = lambda array, r: lax.dynamic_index_in_dim(array, own ^ r, 0, keepdims=False)
    near_mine = jnp.stack(spread_out([pick(by_group, r) for r in range(4)]))
    far_mine = swap(near_mine, 8)
    near_theirs = swap(near_mine, 1)
    far_theirs = swap(far_mine, 1)

    size = lax.axis_size("expert")
    normed_in = normed(state, attention_gain[0])
    blocked = jnp.pad(
        normed_in.reshape(rows, size, width // size), ((0, 0), (0, 0), (0, depth - width // size))
    ).reshape(rows, size * depth)
    tokens = spread_out([blocked] * 4)

    near = pl.pallas_call(
        functools.partial(project_near, depth),
        out_shape=jax.ShapeDtypeStruct((4 * rows, GROUP_COLS), F32),
        in_specs=[SMEM_SPEC] + [VMEM_SPEC] * 6,
        out_specs=VMEM_SPEC,
        compiler_params=params(),
        name="project_near",
    )(where, *tokens, near_mine, near_theirs)
    queries, keyvals = pl.pallas_call(
        functools.partial(project_far, depth),
        out_shape=(
            jax.ShapeDtypeStruct((4, rows, QUERY_COLS), BF16),
            jax.ShapeDtypeStruct((4, rows, 2 * HEAD_DIM), BF16),
        ),
        in_specs=[SMEM_SPEC] + [VMEM_SPEC] * 8,
        out_specs=(VMEM_SPEC, VMEM_SPEC),
        compiler_params=params(),
        name="project_far",
    )(where, *tokens, far_mine, far_theirs, near, bias)

    partner = swap(keyvals, 1)
    rim = lax.ppermute(
        keyvals[3], "expert", [(i, i + 7) for i in range(size - 8) if i & 1]
    )
    behind = jnp.concatenate([rim[None], partner], axis=0)
    attended = pl.pallas_call(
        attend,
        out_shape=jax.ShapeDtypeStruct((4, rows, QUERY_COLS), BF16),
        in_specs=[SMEM_SPEC] + [VMEM_SPEC] * 3 + [SMEM_SPEC],
        out_specs=VMEM_SPEC,
        compiler_params=params(),
        name="attend",
    )(where, queries, keyvals, behind, attention_sink_logits[0])
    heads = jnp.stack(spread_out([pick(attended, r) for r in range(4)]))

    residual, normed_mid = pl.pallas_call(
        out_project,
        out_shape=(jax.ShapeDtypeStruct((rows, width), BF16),) * 2,
        grid_spec=pltpu.PrefetchScalarGridSpec(
            num_scalar_prefetch=1,
            grid=(4,),
            in_specs=[
                pl.BlockSpec((1, rows, QUERY_COLS), lambda r, where: (r, 0, 0)),
                pl.BlockSpec((QUERY_COLS, width), lambda r, where: (where[1] ^ r, 0)),
                pl.BlockSpec((rows, width), lambda r, where: (0, 0)),
                pl.BlockSpec((1, width), lambda r, where: (0, 0)),
                pl.BlockSpec((1, width), lambda r, where: (0, 0)),
            ],
            out_specs=(pl.BlockSpec((rows, width), lambda r, where: (0, 0)),) * 2,
            scratch_shapes=[pltpu.VMEM((rows, width), F32)],
        ),
        compiler_params=params(),
        name="out_project",
    )(where, heads, out_weight[0], state, out_bias, expert_gain)

    gate_up, down = gate_up_weight[0, 0], down_weight[0, 0]
    tiles = [(gate_up, down), (swap(gate_up, 1), swap(down, 1))]
    reach = jnp.stack([placement[0][half * 4 + (own ^ r)] for r in range(4)])
    hot, weight_own = routing(expert_ids[0], gate_logits[0], reach, slots)
    far_hot, weight_far = routing(swap(expert_ids[0], 8), swap(gate_logits[0], 8), reach, slots)

    far_mid = swap(normed_mid, 8)
    near_rows = spread_out(list(packed(hot, normed_mid)))
    far_rows = spread_out(list(packed(far_hot, far_mid)))
    near_out = expert(jnp.stack(near_rows), tiles)
    far_out = expert(jnp.stack(far_rows), tiles)
    far_sum = unpacked(far_hot, weight_far, jnp.stack(spread_out(list(far_out)))).astype(BF16)
    near_sum = unpacked(hot, weight_own, jnp.stack(spread_out(list(near_out))))
    near_sum = (residual.astype(F32) + near_sum).astype(BF16)

    sections = lax.axis_size("section")
    ahead = [
        (s * size + i, (s + 1) % sections * size + (i ^ 8))
        for s in range(sections)
        for i in range(size)
    ]
    far_sum = lax.ppermute(far_sum, ("section", "expert"), ahead)
    near_sum = lax.ppermute(
        near_sum, "section", [(s, (s + 1) % sections) for s in range(sections)]
    )
    return (near_sum.astype(F32) + far_sum.astype(F32)).astype(BF16)[None]


def solution(mesh):
    return jax.shard_map(
        shards,
        mesh=mesh,
        in_specs=(
            P("section", "expert", None),
            P("section", None),
            P("section", "expert", None),
            P("section", None),
            P("section", None, None),
            P("section", None),
            P("section", None),
            P("section", None),
            P("section", "expert", None, None),
            P("section", "expert", None, None),
            P("section", "expert", None),
            P("section", "expert", None),
            P("section", None),
        ),
        out_specs=P("section", "expert", None),
        check_vma=False,
    )
```

time: 663 us -> 323 us (0.49)
  the two profiles are of different devices: /device:TPU:10 before, /device:TPU:0 now
where the time goes in v1:
time: 323 us; the launch traced here: 317 us
  waiting for transfers between devices  165 us (51%)
  matrix products  46 us (14%)
  starting transfers between devices  42.2 us (13%)
  Pallas kernels  28.6 us (9%)
  local copies, waits for them, and re-layouts  25.8 us (8%)
  other arithmetic  8.13 us (3%)
    ppermute x30, waiting for transfers between devices, swap(): return lax.ppermute(x, 'expert', [(i, i ^ mask) for i in range(size)])  133 us
    ppermute x30, starting transfers between devices, swap(): return lax.ppermute(x, 'expert', [(i, i ^ mask) for i in range(size)])  39.2 us
    ppermute x1, waiting for transfers between devices, shards(): far_sum = lax.ppermute(far_sum, ('section', 'expert'), ahead)  32.4 us
    dot_general x4, matrix products, expert(): hidden = jnp.dot(flat, gate_up, preferred_element_type=F32)  23.1 us
    unnamed x29, local copies, waits for them, and re-layouts  18.2 us
    dot_general x4, matrix products, expert(): jnp.dot(swiglu(hidden), down, preferred_element_type=F32).astype(BF16)  16.1 us
    pallas_call x1, Pallas kernels, shards(): pl.pallas_call(attend, out_shape=jax.ShapeDtypeStruct((4, rows, QUERY_COL...  13.1 us
    pallas_call x1, Pallas kernels, shards(): pl.pallas_call(out_project, out_shape=(jax.ShapeDtypeStruct((rows, width)...  7.18 us
  transfers between devices with their start and end apart: 33, of which 18 were waited for; matrix products, arithmetic and copies ran while one was open for 22% of the time, Pallas kernels for 9%

profile of v1, /device:TPU:0, one launch (start us, length us, event | category | flops | bytes accessed | tf_op | source)
XLA Modules:
  0.0 316.7 jit_solution(13788536367101410285)
XLA Ops:
  2.8 3.0 collective-permute-start.3
  8.0 3.8 %collective-permute-done.3 = bf16[192,640]{1,0:T(8,128)(2,1)S(1)} collective-permute-done((bf16[192,640]{1,0:T(8,128)(2,1)S(1)}, bf16[192,640]{1,0:T(8,128)(2,1)S(1)}, u32[]{:S(2)}, u32[]{:S(2)}) %collective-permute-start.3) | collective-permute-done | bytes 245792 | tf_op jit(solution)/shard_map/ppermute | solution.py:25
  11.8 2.9 collective-permute-done.4
  14.7 3.6 %collective-permute-done.5 = bf16[192,640]{1,0:T(8,128)(2,1)S(1)} collective-permute-done((bf16[192,640]{1,0:T(8,128)(2,1)S(1)}, bf16[192,640]{1,0:T(8,128)(2,1)S(1)}, u32[]{:S(2)}, u32[]{:S(2)}) %collective-permute-start.5) | collective-permute-done | bytes 245792 | tf_op jit(solution)/shard_map/ppermute | solution.py:25
  25.4 38.9 %collective-permute-done.6.mine = bf16[4,192,640]{2,1,0:T(8,128)(2,1)} collective-permute-done((bf16[4,192,640]{2,1,0:T(8,128)(2,1)}, bf16[4,192,640]{2,1,0:T(8,128)(2,1)}, u32[]{:S(2)}, u32[]{:S(2)}) %collective-permute-start.6) | collective-permute-done | bytes 983072 | tf_op jit(solution)/shard_map/ppermute | solution.py:25
  67.4 16.3 %copy.74 = bf16[1,2048,2880]{2,1,0:T(8,128)(2,1)} copy(bf16[1,2048,2880]{1,2,0:T(8,128)(2,1)} %param.17) | data formatting | bytes 23592960 | tf_op args[4]
  89.3 12.8 %collective-permute-done.2.t3 = bf16[128,3072]{1,0:T(8,128)(2,1)} collective-permute-done((bf16[128,3072]{1,0:T(8,128)(2,1)S(1)}, bf16[128,3072]{1,0:T(8,128)(2,1)}, u32[]{:S(2)}, u32[]{:S(2)}) %collective-permute-start.2) | collective-permute-done | bytes 786464 | tf_op jit(solution)/shard_map/ppermute | solution.py:25
  104.4 4.5 %project_near.1.near = f32[512,640]{1,0:T(8,128)} custom-call(s32[3]{0:T(128)S(1)} %pad_add_fusion.where, bf16[128,3072]{1,0:T(8,128)(2,1)S(1)} %copy.73.t0, bf16[128,3072]{1,0:T(8,128)(2,1)S(1)} %collective-permute-done.t1, bf16[128,3072]{1,0:T(8,128)(2,1)S(1)} %collective-permute-done.1.t2, bf16[128,3072]{1,0:T(8,128)(2,1)} %collective-permute-done.2.t3, ...), custom_call_target="tpu_custom_call" | custom-call | tf_op jit(solution)/shard_map/project_near/pallas_call | solution.py:233
  108.8 3.8 %project_far.1 = (bf16[4,128,512]{2,1,0:T(8,128)(2,1)S(1)}, bf16[4,128,128]{2,1,0:T(8,128)(2,1)S(1)}) custom-call(s32[3]{0:T(128)S(1)} %pad_add_fusion.where, bf16[128,3072]{1,0:T(8,128)(2,1)S(1)} %copy.73.t0, bf16[128,3072]{1,0:T(8,128)(2,1)S(1)} %collective-permute-done.t1, bf16[128,3072]{1,0:T(8,128)(2,1)S(1)} %collective-permute-done.1.t2, ...), custom_call_target="tpu_custom_call" | custom-call | tf_op jit(solution)/shard_map/project_far/pallas_call | solution.py:241
  114.1 13.1 %attend.1 = bf16[4,128,512]{2,1,0:T(8,128)(2,1)S(1)} custom-call(s32[3]{0:T(128)S(1)} %pad_add_fusion.where, bf16[4,128,512]{2,1,0:T(8,128)(2,1)S(1)} %get-tuple-element.9.queries, bf16[4,128,128]{2,1,0:T(8,128)(2,1)S(1)} %get-tuple-element.10.keyvals, bf16[5,128,128]{2,1,0:T(8,128)(2,1)S(1)} %pad_maximum_fusion.4.behind, f32[32]{0:T(128)S(1)} %bitcast.107), custom_call_target="tpu_custom_call" | custom-call | tf_op jit(solution)/shard_map/attend/pallas_call | solution.py:258
  133.2 3.8 %collective-permute-done.13 = bf16[128,512]{1,0:T(8,128)(2,1)S(1)} collective-permute-done((bf16[128,512]{1,0:T(8,128)(2,1)S(1)}, bf16[128,512]{1,0:T(8,128)(2,1)S(1)}, u32[]{:S(2)}, u32[]{:S(2)}) %collective-permute-start.13) | collective-permute-done | bytes 131104 | tf_op jit(solution)/shard_map/ppermute | solution.py:25
  137.0 7.2 %out_project.1 = (bf16[128,2880]{1,0:T(8,128)(2,1)S(1)}, bf16[128,2880]{1,0:T(8,128)(2,1)S(1)}) custom-call(s32[3]{0:T(128)S(1)} %pad_add_fusion.where, bf16[4,128,512]{2,1,0:T(8,128)(2,1)S(1)} %pad_maximum_fusion.3.attended, bf16[2048,2880]{1,0:T(8,128)(2,1)} %bitcast.108, bf16[128,2880]{1,0:T(8,128)(2,1)S(1)} %bitcast.106, f32[1,2880]{1,0:T(1,128)S(1)} %copy-done, ...), custom_call_target="tpu_custom_call" | custom-call | tf_op jit(solution)/shard_map/out_project/pallas_call | solution.py:268
  150.5 9.4 %collective-permute-done.14 = bf16[80,2880]{1,0:T(8,128)(2,1)} collective-permute-done((bf16[80,2880]{1,0:T(8,128)(2,1)}, bf16[80,2880]{1,0:T(8,128)(2,1)}, u32[]{:S(2)}, u32[]{:S(2)}) %collective-permute-start.14) | collective-permute-done | bytes 460832 | tf_op jit(solution)/shard_map/ppermute | solution.py:25
  159.8 3.0 collective-permute-start.24
  162.8 15.2 %collective-permute-done.16 = bf16[80,2880]{1,0:T(8,128)(2,1)} collective-permute-done((bf16[80,2880]{1,0:T(8,128)(2,1)S(1)}, bf16[80,2880]{1,0:T(8,128)(2,1)}, u32[]{:S(2)}, u32[]{:S(2)}) %collective-permute-start.16) | collective-permute-done | bytes 460832 | tf_op jit(solution)/shard_map/ppermute | solution.py:25
  179.7 8.0 %fusion.76 = f32[320,1440]{1,0:T(8,128)} fusion(bf16[320,2880]{1,0:T(8,128)(2,1)S(1)} %bitcast.113, bf16[1,1,2880,1440]{2,3,1,0:T(8,128)(2,1)} %param.21), kind=kOutput, calls=%fused_computation.130 | convolution fusion | flops 2654208000 | bytes 11980800 | tf_op jit(solution)/shard_map/dot_general | solution.py:168
  187.6 7.4 %collective-permute-done.24 = bf16[128,2880]{0,1:T(8,128)(2,1)S(1)} collective-permute-done((bf16[128,2880]{0,1:T(8,128)(2,1)S(1)}, bf16[128,2880]{0,1:T(8,128)(2,1)S(1)}, u32[]{:S(2)}, u32[]{:S(2)}) %collective-permute-start.24) | collective-permute-done | bytes 737312 | tf_op jit(solution)/shard_map/ppermute | solution.py:25
  196.0 3.4 %collective-permute-start.27 = (bf16[80,2880]{1,0:T(8,128)(2,1)S(1)}, bf16[80,2880]{1,0:T(8,128)(2,1)S(1)}, u32[]{:S(2)}, u32[]{:S(2)}) collective-permute-start(bf16[80,2880]{1,0:T(8,128)(2,1)S(1)} %get-tuple-element.32), channel_id=1, source_target_pairs={{0,6},{1,7},{2,4},{3,5},{4,2},{5,3},{6,0},{7,1},{8,14},{9,15},{10,... | collective-permute-start | bytes 1382408 | tf_op jit(solution)/shard_map/ppermute | solution.py:25
  199.4 4.0 %fusion.7 = f32[320,2880]{1,0:T(8,128)S(1)} fusion(f32[320,1440]{1,0:T(8,128)S(1)} %copy-done.9, bf16[1,1,720,2880]{3,2,1,0:T(8,128)(2,1)} %param.22), kind=kOutput, calls=%fused_computation.14 | convolution fusion | flops 1330790400 | bytes 9676800 | tf_op jit(solution)/shard_map/dot_general | solution.py:169
  203.4 5.3 %collective-permute-done.25 = bf16[80,2880]{1,0:T(8,128)(2,1)S(1)} collective-permute-done((bf16[80,2880]{1,0:T(8,128)(2,1)S(1)}, bf16[80,2880]{1,0:T(8,128)(2,1)S(1)}, u32[]{:S(2)}, u32[]{:S(2)}) %collective-permute-start.25) | collective-permute-done | bytes 460832 | tf_op jit(solution)/shard_map/ppermute | solution.py:25
  209.7 9.5 %collective-permute-done.27 = bf16[80,2880]{1,0:T(8,128)(2,1)S(1)} collective-permute-done((bf16[80,2880]{1,0:T(8,128)(2,1)S(1)}, bf16[80,2880]{1,0:T(8,128)(2,1)S(1)}, u32[]{:S(2)}, u32[]{:S(2)}) %collective-permute-start.27) | collective-permute-done | bytes 460832 | tf_op jit(solution)/shard_map/ppermute | solution.py:25
  219.5 3.2 %fusion.74 = f32[320,1440]{1,0:T(8,128)S(1)} fusion(bf16[320,2880]{1,0:T(8,128)(2,1)S(1)} %bitcast.115, bf16[1,1,2880,1440]{2,3,1,0:T(8,128)(2,1)S(1)} %bitcast.135), kind=kOutput, calls=%fused_computation.128 | convolution fusion | flops 2654208000 | bytes 11980800 | tf_op jit(solution)/shard_map/dot_general | solution.py:168
  222.8 4.0 %fusion.3 = f32[320,2880]{1,0:T(8,128)S(1)} fusion(f32[320,1440]{1,0:T(8,128)S(1)} %fusion.74, bf16[1,1,720,2880]{3,2,1,0:T(8,128)(2,1)} %param.22), kind=kOutput, calls=%fused_computation.7 | convolution fusion | flops 1330790400 | bytes 9676800 | tf_op jit(solution)/shard_map/dot_general | solution.py:169
  226.8 6.1 %fusion.89 = f32[320,1440]{1,0:T(8,128)S(1)} fusion(bf16[320,2880]{1,0:T(8,128)(2,1)S(1)} %bitcast.114, bf16[2880,1440]{0,1:T(8,128)(2,1)} %collective-permute-done.17), kind=kOutput, calls=%fused_computation.143 | convolution fusion | flops 2654208000 | bytes 11980800 | tf_op jit(solution)/shard_map/dot_general | solution.py:168
  232.9 4.0 %fusion.6 = bf16[320,2880]{1,0:T(8,128)(2,1)S(1)} fusion(f32[320,2880]{1,0:T(8,128)S(1)} %fusion.7, bf16[720,2880]{1,0:T(8,128)(2,1)} %collective-permute-done.18, f32[320,1440]{1,0:T(8,128)S(1)} %fusion.89), kind=kOutput, calls=%fused_computation.12 | convolution fusion | flops 1332633600 | bytes 11520000 | tf_op jit(solution)/shard_map/dot_general | solution.py:169
  240.6 5.8 %fusion.90 = f32[320,1440]{1,0:T(8,128)S(1)} fusion(bf16[320,2880]{1,0:T(8,128)(2,1)S(1)} %bitcast.116, bf16[2880,1440]{0,1:T(8,128)(2,1)} %collective-permute-done.17), kind=kOutput, calls=%fused_computation.144 | convolution fusion | flops 2654208000 | bytes 11980800 | tf_op jit(solution)/shard_map/dot_general | solution.py:168
  246.4 4.1 %fusion.2 = bf16[320,2880]{1,0:T(8,128)(2,1)S(1)} fusion(f32[320,2880]{1,0:T(8,128)S(1)} %fusion.3, bf16[720,2880]{1,0:T(8,128)(2,1)} %collective-permute-done.18, f32[320,1440]{1,0:T(8,128)S(1)} %fusion.90), kind=kOutput, calls=%fused_computation.5 | convolution fusion | flops 1332633600 | bytes 11520000 | tf_op jit(solution)/shard_map/dot_general | solution.py:169
  252.3 2.8 collective-permute-start.30
  255.1 7.3 %collective-permute-done.21 = bf16[80,2880]{1,0:T(8,128)(2,1)S(1)} collective-permute-done((bf16[80,2880]{1,0:T(8,128)(2,1)S(1)}, bf16[80,2880]{1,0:T(8,128)(2,1)S(1)}, u32[]{:S(2)}, u32[]{:S(2)}) %collective-permute-start.21) | collective-permute-done | bytes 460832 | tf_op jit(solution)/shard_map/ppermute | solution.py:25
  268.8 3.2 collective-permute-done.28
  272.0 7.5 %collective-permute-done.30 = bf16[80,2880]{1,0:T(8,128)(2,1)} collective-permute-done((bf16[80,2880]{1,0:T(8,128)(2,1)}, bf16[80,2880]{1,0:T(8,128)(2,1)}, u32[]{:S(2)}, u32[]{:S(2)}) %collective-permute-start.30) | collective-permute-done | bytes 460832 | tf_op jit(solution)/shard_map/ppermute | solution.py:25
  282.8 32.4 %collective-permute-done.32 = bf16[128,2880]{0,1:T(8,128)(2,1)S(1)} collective-permute-done((bf16[128,2880]{0,1:T(8,128)(2,1)S(1)}, bf16[128,2880]{0,1:T(8,128)(2,1)S(1)}, u32[]{:S(2)}, u32[]{:S(2)}) %collective-permute-start.32) | collective-permute-done | bytes 737312 | tf_op jit(solution)/shard_map/ppermute | solution.py:309
  (130 shorter events, 56.4 us)
Async XLA Ops:
  2.8 9.0 %collective-permute-start.3 = (bf16[192,640]{1,0:T(8,128)(2,1)S(1)}, bf16[192,640]{1,0:T(8,128)(2,1)S(1)}, u32[]{:S(2)}, u32[]{:S(2)}) collective-permute-start(bf16[192,640]{1,0:T(8,128)(2,1)S(1)} %get-tuple-element.38), channel_id=1, source_target_pairs={{0,2},{1,3},{2,0},{3,1},{4,6},{5,7},{6,4},{7,5},{8,10},{9,11},{10,... | collective-permute-start | bytes 737288 | tf_op jit(solution)/shard_map/ppermute | solution.py:25
  5.8 8.9 %collective-permute-start.4 = (bf16[192,640]{1,0:T(8,128)(2,1)S(1)}, bf16[192,640]{1,0:T(8,128)(2,1)S(1)}, u32[]{:S(2)}, u32[]{:S(2)}) collective-permute-start(bf16[192,640]{1,0:T(8,128)(2,1)S(1)} %get-tuple-element.39), channel_id=1, source_target_pairs={{0,4},{1,5},{2,6},{3,7},{4,0},{5,1},{6,2},{7,3},{8,12},{9,13},{10,... | collective-permute-start | bytes 737288 | tf_op jit(solution)/shard_map/ppermute | solution.py:25
  7.4 10.9 %collective-permute-start.5 = (bf16[192,640]{1,0:T(8,128)(2,1)S(1)}, bf16[192,640]{1,0:T(8,128)(2,1)S(1)}, u32[]{:S(2)}, u32[]{:S(2)}) collective-permute-start(bf16[192,640]{1,0:T(8,128)(2,1)S(1)} %get-tuple-element.40), channel_id=1, source_target_pairs={{0,6},{1,7},{2,4},{3,5},{4,2},{5,3},{6,0},{7,1},{8,14},{9,15},{10,... | collective-permute-start | bytes 737288 | tf_op jit(solution)/shard_map/ppermute | solution.py:25
  19.4 44.9 %collective-permute-start.6 = (bf16[4,192,640]{2,1,0:T(8,128)(2,1)}, bf16[4,192,640]{2,1,0:T(8,128)(2,1)}, u32[]{:S(2)}, u32[]{:S(2)}) collective-permute-start(bf16[4,192,640]{2,1,0:T(8,128)(2,1)} %pad_maximum_fusion.2.mine), channel_id=1, source_target_pairs={{0,8},{1,9},{2,10},{3,11},{4,12},{5,13},{6,14},{7,15},{8,0},{9,1},... | collective-permute-start | bytes 2949128 | tf_op jit(solution)/shard_map/ppermute | solution.py:25
  23.3 41.7 %collective-permute-start = (bf16[128,3072]{1,0:T(8,128)(2,1)S(1)}, bf16[128,3072]{1,0:T(8,128)(2,1)S(1)}, u32[]{:S(2)}, u32[]{:S(2)}) collective-permute-start(bf16[128,3072]{1,0:T(8,128)(2,1)S(1)} %copy.73.t0), channel_id=1, source_target_pairs={{0,2},{1,3},{2,0},{3,1},{4,6},{5,7},{6,4},{7,5},{8,10},{9,11},{10,... | collective-permute-start | bytes 2359304 | tf_op jit(solution)/shard_map/ppermute | solution.py:25
  24.9 201.9 %collective-permute-start.17 = (bf16[2880,1440]{0,1:T(8,128)(2,1)}, bf16[2880,1440]{0,1:T(8,128)(2,1)}, u32[]{:S(2)}, u32[]{:S(2)}) collective-permute-start(bf16[2880,1440]{0,1:T(8,128)(2,1)} %bitcast.133), channel_id=1, source_target_pairs={{0,1},{1,0},{2,3},{3,2},{4,5},{5,4},{6,7},{7,6},{8,9},{9,8},{10,11... | collective-permute-start | bytes 24883208 | tf_op jit(solution)/shard_map/ppermute | solution.py:25
  24.9 79.5 %collective-permute-start.8 = (bf16[4,192,640]{2,1,0:T(8,128)(2,1)}, bf16[4,192,640]{2,1,0:T(8,128)(2,1)}, u32[]{:S(2)}, u32[]{:S(2)}) collective-permute-start(bf16[4,192,640]{2,1,0:T(8,128)(2,1)} %pad_maximum_fusion.2.mine), channel_id=1, source_target_pairs={{0,1},{1,0},{2,3},{3,2},{4,5},{5,4},{6,7},{7,6},{8,9},{9,8},{10,11... | collective-permute-start | bytes 2949128 | tf_op jit(solution)/shard_map/ppermute | solution.py:25
  64.3 44.5 %collective-permute-start.7 = (bf16[4,192,640]{2,1,0:T(8,128)(2,1)}, bf16[4,192,640]{2,1,0:T(8,128)(2,1)}, u32[]{:S(2)}, u32[]{:S(2)}) collective-permute-start(bf16[4,192,640]{2,1,0:T(8,128)(2,1)} %collective-permute-done.6.mine), channel_id=1, source_target_pairs={{0,1},{1,0},{2,3},{3,2},{4,5},{5,4},{6,7},{7,6},{8,9},{9,8},{10,11... | collective-permute-start | bytes 2949128 | tf_op jit(solution)/shard_map/ppermute | solution.py:25
  64.3 22.8 %collective-permute-start.1 = (bf16[128,3072]{1,0:T(8,128)(2,1)S(1)}, bf16[128,3072]{1,0:T(8,128)(2,1)S(1)}, u32[]{:S(2)}, u32[]{:S(2)}) collective-permute-start(bf16[128,3072]{1,0:T(8,128)(2,1)S(1)} %copy.73.t0), channel_id=1, source_target_pairs={{0,4},{1,5},{2,6},{3,7},{4,0},{5,1},{6,2},{7,3},{8,12},{9,13},{10,... | collective-permute-start | bytes 2359304 | tf_op jit(solution)/shard_map/ppermute | solution.py:25
  65.1 37.0 %collective-permute-start.2 = (bf16[128,3072]{1,0:T(8,128)(2,1)S(1)}, bf16[128,3072]{1,0:T(8,128)(2,1)}, u32[]{:S(2)}, u32[]{:S(2)}) collective-permute-start(bf16[128,3072]{1,0:T(8,128)(2,1)S(1)} %copy.73.t0), channel_id=1, source_target_pairs={{0,6},{1,7},{2,4},{3,5},{4,2},{5,3},{6,0},{7,1},{8,14},{9,15},{10,... | collective-permute-start | bytes 2359304 | tf_op jit(solution)/shard_map/ppermute | solution.py:25
  87.1 26.5 %collective-permute-start.23 = (s32[128,4]{0,1:T(4,128)S(1)}, s32[128,4]{0,1:T(4,128)S(1)}, u32[]{:S(2)}, u32[]{:S(2)}) collective-permute-start(s32[128,4]{0,1:T(4,128)S(1)} %bitcast.130), channel_id=1, source_target_pairs={{0,8},{1,9},{2,10},{3,11},{4,12},{5,13},{6,14},{7,15},{8,0},{9,1},... | collective-permute-start | bytes 6152 | tf_op jit(solution)/shard_map/ppermute | solution.py:25
  102.1 28.9 %collective-permute-start.31 = (f32[128,4]{0,1:T(4,128)S(1)}, f32[128,4]{0,1:T(4,128)S(1)}, u32[]{:S(2)}, u32[]{:S(2)}) collective-permute-start(f32[128,4]{0,1:T(4,128)S(1)} %bitcast.129), channel_id=1, source_target_pairs={{0,8},{1,9},{2,10},{3,11},{4,12},{5,13},{6,14},{7,15},{8,0},{9,1},... | collective-permute-start | bytes 6152 | tf_op jit(solution)/shard_map/ppermute | solution.py:25
  112.7 1.4 collective-permute-start.10
  127.3 5.3 %collective-permute-start.11 = (bf16[128,512]{1,0:T(8,128)(2,1)S(1)}, bf16[128,512]{1,0:T(8,128)(2,1)S(1)}, u32[]{:S(2)}, u32[]{:S(2)}) collective-permute-start(bf16[128,512]{1,0:T(8,128)(2,1)S(1)} %get-tuple-element.44), channel_id=1, source_target_pairs={{0,2},{1,3},{2,0},{3,1},{4,6},{5,7},{6,4},{7,5},{8,10},{9,11},{10,... | collective-permute-start | bytes 393224 | tf_op jit(solution)/shard_map/ppermute | solution.py:25
  127.9 5.3 %collective-permute-start.12 = (bf16[128,512]{1,0:T(8,128)(2,1)S(1)}, bf16[128,512]{1,0:T(8,128)(2,1)S(1)}, u32[]{:S(2)}, u32[]{:S(2)}) collective-permute-start(bf16[128,512]{1,0:T(8,128)(2,1)S(1)} %get-tuple-element.43), channel_id=1, source_target_pairs={{0,4},{1,5},{2,6},{3,7},{4,0},{5,1},{6,2},{7,3},{8,12},{9,13},{10,... | collective-permute-start | bytes 393224 | tf_op jit(solution)/shard_map/ppermute | solution.py:25
  129.7 7.3 %collective-permute-start.13 = (bf16[128,512]{1,0:T(8,128)(2,1)S(1)}, bf16[128,512]{1,0:T(8,128)(2,1)S(1)}, u32[]{:S(2)}, u32[]{:S(2)}) collective-permute-start(bf16[128,512]{1,0:T(8,128)(2,1)S(1)} %get-tuple-element.42), channel_id=1, source_target_pairs={{0,6},{1,7},{2,4},{3,5},{4,2},{5,3},{6,0},{7,1},{8,14},{9,15},{10,... | collective-permute-start | bytes 393224 | tf_op jit(solution)/shard_map/ppermute | solution.py:25
  131.0 101.9 %collective-permute-start.18 = (bf16[720,2880]{1,0:T(8,128)(2,1)}, bf16[720,2880]{1,0:T(8,128)(2,1)}, u32[]{:S(2)}, u32[]{:S(2)}) collective-permute-start(bf16[720,2880]{1,0:T(8,128)(2,1)} %bitcast.41), channel_id=1, source_target_pairs={{0,1},{1,0},{2,3},{3,2},{4,5},{5,4},{6,7},{7,6},{8,9},{9,8},{10,11... | collective-permute-start | bytes 12441608 | tf_op jit(solution)/shard_map/ppermute | solution.py:25
  145.9 13.9 %collective-permute-start.14 = (bf16[80,2880]{1,0:T(8,128)(2,1)}, bf16[80,2880]{1,0:T(8,128)(2,1)}, u32[]{:S(2)}, u32[]{:S(2)}) collective-permute-start(bf16[80,2880]{1,0:T(8,128)(2,1)} %get-tuple-element.26), channel_id=1, source_target_pairs={{0,2},{1,3},{2,0},{3,1},{4,6},{5,7},{6,4},{7,5},{8,10},{9,11},{10,... | collective-permute-start | bytes 1382408 | tf_op jit(solution)/shard_map/ppermute | solution.py:25
  147.5 15.3 %collective-permute-start.15 = (bf16[80,2880]{1,0:T(8,128)(2,1)}, bf16[80,2880]{1,0:T(8,128)(2,1)}, u32[]{:S(2)}, u32[]{:S(2)}) collective-permute-start(bf16[80,2880]{1,0:T(8,128)(2,1)} %get-tuple-element.25), channel_id=1, source_target_pairs={{0,4},{1,5},{2,6},{3,7},{4,0},{5,1},{6,2},{7,3},{8,12},{9,13},{10,... | collective-permute-start | bytes 1382408 | tf_op jit(solution)/shard_map/ppermute | solution.py:25
  148.9 29.1 %collective-permute-start.16 = (bf16[80,2880]{1,0:T(8,128)(2,1)S(1)}, bf16[80,2880]{1,0:T(8,128)(2,1)}, u32[]{:S(2)}, u32[]{:S(2)}) collective-permute-start(bf16[80,2880]{1,0:T(8,128)(2,1)S(1)} %get-tuple-element.24), channel_id=1, source_target_pairs={{0,6},{1,7},{2,4},{3,5},{4,2},{5,3},{6,0},{7,1},{8,14},{9,15},{10,... | collective-permute-start | bytes 1382408 | tf_op jit(solution)/shard_map/ppermute | solution.py:25
  159.8 35.1 %collective-permute-start.24 = (bf16[128,2880]{0,1:T(8,128)(2,1)S(1)}, bf16[128,2880]{0,1:T(8,128)(2,1)S(1)}, u32[]{:S(2)}, u32[]{:S(2)}) collective-permute-start(bf16[128,2880]{0,1:T(8,128)(2,1)S(1)} %copy.78), channel_id=1, source_target_pairs={{0,8},{1,9},{2,10},{3,11},{4,12},{5,13},{6,14},{7,15},{8,0},{9,1},... | collective-permute-start | bytes 2211848 | tf_op jit(solution)/shard_map/ppermute | solution.py:25
  195.8 12.9 %collective-permute-start.25 = (bf16[80,2880]{1,0:T(8,128)(2,1)S(1)}, bf16[80,2880]{1,0:T(8,128)(2,1)S(1)}, u32[]{:S(2)}, u32[]{:S(2)}) collective-permute-start(bf16[80,2880]{1,0:T(8,128)(2,1)S(1)} %get-tuple-element.34), channel_id=1, source_target_pairs={{0,2},{1,3},{2,0},{3,1},{4,6},{5,7},{6,4},{7,5},{8,10},{9,11},{10,... | collective-permute-start | bytes 1382408 | tf_op jit(solution)/shard_map/ppermute | solution.py:25
  195.9 13.8 %collective-permute-start.26 = (bf16[80,2880]{1,0:T(8,128)(2,1)S(1)}, bf16[80,2880]{1,0:T(8,128)(2,1)S(1)}, u32[]{:S(2)}, u32[]{:S(2)}) collective-permute-start(bf16[80,2880]{1,0:T(8,128)(2,1)S(1)} %get-tuple-element.33), channel_id=1, source_target_pairs={{0,4},{1,5},{2,6},{3,7},{4,0},{5,1},{6,2},{7,3},{8,12},{9,13},{10,... | collective-permute-start | bytes 1382408 | tf_op jit(solution)/shard_map/ppermute | solution.py:25
  196.0 23.2 %collective-permute-start.27 = (bf16[80,2880]{1,0:T(8,128)(2,1)S(1)}, bf16[80,2880]{1,0:T(8,128)(2,1)S(1)}, u32[]{:S(2)}, u32[]{:S(2)}) collective-permute-start(bf16[80,2880]{1,0:T(8,128)(2,1)S(1)} %get-tuple-element.32), channel_id=1, source_target_pairs={{0,6},{1,7},{2,4},{3,5},{4,2},{5,3},{6,0},{7,1},{8,14},{9,15},{10,... | collective-permute-start | bytes 1382408 | tf_op jit(solution)/shard_map/ppermute | solution.py:25
  237.0 15.2 %collective-permute-start.19 = (bf16[80,2880]{1,0:T(8,128)(2,1)S(1)}, bf16[80,2880]{1,0:T(8,128)(2,1)S(1)}, u32[]{:S(2)}, u32[]{:S(2)}) collective-permute-start(bf16[80,2880]{1,0:T(8,128)(2,1)S(1)} %get-tuple-element.22), channel_id=1, source_target_pairs={{0,2},{1,3},{2,0},{3,1},{4,6},{5,7},{6,4},{7,5},{8,10},{9,11},{10,... | collective-permute-start | bytes 1382408 | tf_op jit(solution)/shard_map/ppermute | solution.py:25
  237.5 17.7 %collective-permute-start.20 = (bf16[80,2880]{1,0:T(8,128)(2,1)S(1)}, bf16[80,2880]{1,0:T(8,128)(2,1)S(1)}, u32[]{:S(2)}, u32[]{:S(2)}) collective-permute-start(bf16[80,2880]{1,0:T(8,128)(2,1)S(1)} %get-tuple-element.21), channel_id=1, source_target_pairs={{0,4},{1,5},{2,6},{3,7},{4,0},{5,1},{6,2},{7,3},{8,12},{9,13},{10,... | collective-permute-start | bytes 1382408 | tf_op jit(solution)/shard_map/ppermute | solution.py:25
  237.7 24.7 %collective-permute-start.21 = (bf16[80,2880]{1,0:T(8,128)(2,1)S(1)}, bf16[80,2880]{1,0:T(8,128)(2,1)S(1)}, u32[]{:S(2)}, u32[]{:S(2)}) collective-permute-start(bf16[80,2880]{1,0:T(8,128)(2,1)S(1)} %get-tuple-element.20), channel_id=1, source_target_pairs={{0,6},{1,7},{2,4},{3,5},{4,2},{5,3},{6,0},{7,1},{8,14},{9,15},{10,... | collective-permute-start | bytes 1382408 | tf_op jit(solution)/shard_map/ppermute | solution.py:25
  251.6 20.3 %collective-permute-start.28 = (bf16[80,2880]{1,0:T(8,128)(2,1)}, bf16[80,2880]{1,0:T(8,128)(2,1)}, u32[]{:S(2)}, u32[]{:S(2)}) collective-permute-start(bf16[80,2880]{1,0:T(8,128)(2,1)} %get-tuple-element.30), channel_id=1, source_target_pairs={{0,2},{1,3},{2,0},{3,1},{4,6},{5,7},{6,4},{7,5},{8,10},{9,11},{10,... | collective-permute-start | bytes 1382408 | tf_op jit(solution)/shard_map/ppermute | solution.py:25
  252.0 20.0 %collective-permute-start.29 = (bf16[80,2880]{1,0:T(8,128)(2,1)}, bf16[80,2880]{1,0:T(8,128)(2,1)}, u32[]{:S(2)}, u32[]{:S(2)}) collective-permute-start(bf16[80,2880]{1,0:T(8,128)(2,1)} %get-tuple-element.29), channel_id=1, source_target_pairs={{0,4},{1,5},{2,6},{3,7},{4,0},{5,1},{6,2},{7,3},{8,12},{9,13},{10,... | collective-permute-start | bytes 1382408 | tf_op jit(solution)/shard_map/ppermute | solution.py:25
  252.3 27.2 %collective-permute-start.30 = (bf16[80,2880]{1,0:T(8,128)(2,1)}, bf16[80,2880]{1,0:T(8,128)(2,1)}, u32[]{:S(2)}, u32[]{:S(2)}) collective-permute-start(bf16[80,2880]{1,0:T(8,128)(2,1)} %get-tuple-element.28), channel_id=1, source_target_pairs={{0,6},{1,7},{2,4},{3,5},{4,2},{5,3},{6,0},{7,1},{8,14},{9,15},{10,... | collective-permute-start | bytes 1382408 | tf_op jit(solution)/shard_map/ppermute | solution.py:25
  267.2 15.6 %collective-permute-start.22 = (bf16[128,2880]{0,1:T(8,128)(2,1)S(1)}, bf16[128,2880]{0,1:T(8,128)(2,1)S(1)}, u32[]{:S(2)}, u32[]{:S(2)}) collective-permute-start(bf16[128,2880]{0,1:T(8,128)(2,1)S(1)} %copy.77), channel_id=1, source_target_pairs={{0,16},{16,0},{1,17},{17,1},{2,18},{18,2},{3,19},{19,3},{4,20},{20... | collective-permute-start | bytes 2211848 | tf_op jit(solution)/shard_map/ppermute | solution.py:310
  282.2 33.0 %collective-permute-start.32 = (bf16[128,2880]{0,1:T(8,128)(2,1)S(1)}, bf16[128,2880]{0,1:T(8,128)(2,1)S(1)}, u32[]{:S(2)}, u32[]{:S(2)}) collective-permute-start(bf16[128,2880]{0,1:T(8,128)(2,1)S(1)} %multiply_reduce_fusion), channel_id=1, source_target_pairs={{0,24},{1,25},{2,26},{3,27},{4,28},{5,29},{6,30},{7,31},{8,16},{9,... | collective-permute-start | bytes 2211848 | tf_op jit(solution)/shard_map/ppermute | solution.py:309
  (14 other events, 230.6 us)
